TPU v7x, 32 devices: a whole 2x2x4 slice. The times are simulated.
32 devices in a mesh: grp: 4 (over z), ep: 8 (over y, x, core).
Axes of the slice: x: 2, y: 2, z: 4, core: 2. Of those that a mesh axis runs over, the one named last changes fastest.
Arguments:
- tokens: bfloat16 [4096, 2048], P(('grp', 'ep')), may hold values from -6 to 6
- norm_gain: float32 [2048], replicated, may hold values from 0.25 to 1.75
- w_gate: bfloat16 [8, 2048, 512], P('ep', 'grp'), may hold values from -0.125 to 0.125
- w_up: bfloat16 [8, 2048, 512], P('ep', 'grp'), may hold values from -0.125 to 0.125
- w_down: bfloat16 [8, 512, 2048], P('ep', None, 'grp'), may hold values from -0.25 to 0.25
- expert_ids: int32 [4096, 2], P(('grp', 'ep')), may hold values from 0 to 7, all different within a row; in each aligned block of 128 rows (0 to 127, 128 to 255, ...) at most 48 rows name the same one
- probs: float32 [4096, 2], P(('grp', 'ep')), may hold values from 0.1 to 1
- out_grad: bfloat16 [4096, 2048], P(('grp', 'ep')), may hold values from -6 to 6
Outputs:
- grad_tokens: bfloat16 [4096, 2048], P(('grp', 'ep'))
- grad_up: float32 [8, 2048, 512], P('ep', 'grp')
- grad_down: float32 [8, 512, 2048], P('ep', None, 'grp')
Inputs may be any that keep to these rules, and one draw needn't show every extreme that they name: `expert_ids`: each row names 2 different experts; among the 128 rows of one device, no expert is named by more than 48 rows, a bound that some block reaches.
All inputs are finite; a program needn't handle non-finite values.
Results may differ from a plain program's by a relative error of at most 0.017.
Values may be sent and summed in bfloat16 or wider, within the bound.
A program may use at most 64 MiB of HBM per device.

v0:
```python
import math

import jax
import jax.numpy as jnp
from jax import lax
from jax.sharding import PartitionSpec as P

EPS = 1e-06


def forward_part(hidden_rows, gate_full, up_full):
    pre_gate = jnp.dot(hidden_rows, gate_full, preferred_element_type=jnp.float32)
    pre_up = jnp.dot(hidden_rows, up_full, preferred_element_type=jnp.float32)
    return (pre_gate, pre_up)


def backward_part(hidden_rows, cot_rows, pre_gate, pre_up, gate_full, up_full, down_full):
    sigmoid_gate = jax.nn.sigmoid(pre_gate)
    act_gate = pre_gate * sigmoid_gate
    swiglu = (act_gate * pre_up).astype(jnp.bfloat16)
    d_swiglu = jnp.einsum("rd,fd->rf", cot_rows, down_full, preferred_element_type=jnp.float32)
    d_up_pre = (d_swiglu * act_gate).astype(jnp.bfloat16)
    d_gate_pre = (
        d_swiglu * pre_up * sigmoid_gate * (1.0 + pre_gate * (1.0 - sigmoid_gate))
    ).astype(jnp.bfloat16)
    d_hidden = jnp.einsum("rf,df->rd", d_gate_pre, gate_full, preferred_element_type=jnp.float32)
    d_hidden = (
        d_hidden + jnp.einsum("rf,df->rd", d_up_pre, up_full, preferred_element_type=jnp.float32)
    ).astype(jnp.bfloat16)
    part_up = jnp.einsum("rd,rf->df", hidden_rows, d_up_pre, preferred_element_type=jnp.float32)
    part_down = jnp.einsum("rf,rd->fd", swiglu, cot_rows, preferred_element_type=jnp.float32)
    return (d_hidden, part_up, part_down)


def shards(tokens, norm_gain, w_gate, w_up, w_down, expert_ids, probs, out_grad):
    row_count, width = tokens.shape
    top_count = expert_ids.shape[1]
    expert_count = lax.axis_size("ep") * w_gate.shape[0]
    capacity = max(2, 3 * row_count * top_count // (2 * expert_count))
    entry_total = row_count * top_count
    token_f = tokens.astype(jnp.float32)
    inverse = lax.rsqrt(jnp.mean(token_f * token_f, axis=1, keepdims=True) + EPS)
    normed = token_f * inverse
    hidden = (normed * norm_gain[None, :]).astype(jnp.bfloat16)
    weighted = (probs[:, :, None] * out_grad.astype(jnp.float32)[:, None, :]).astype(jnp.bfloat16)
    weighted = weighted.reshape(entry_total, width)
    flat_ids = expert_ids.reshape(-1)
    onehot = (flat_ids[:, None] == jnp.arange(expert_count, dtype=jnp.int32)[None, :]).astype(
        jnp.int32
    )
    position = jnp.sum((jnp.cumsum(onehot, axis=0) - 1) * onehot, axis=1)
    target = flat_ids * capacity + position
    source = jnp.full((expert_count * capacity,), entry_total, jnp.int32)
    source = source.at[target].set(jnp.arange(entry_total, dtype=jnp.int32))
    hidden_pad = jnp.concatenate([hidden, jnp.zeros((1, width), jnp.bfloat16)], axis=0)
    weighted_pad = jnp.concatenate([weighted, jnp.zeros((1, width), jnp.bfloat16)], axis=0)
    hidden_send = hidden_pad[source // top_count].reshape(expert_count, capacity, width)
    cot_send = weighted_pad[source].reshape(expert_count, capacity, width)
    gate_full, up_full, down_full = (
        lax.all_gather(w_gate, "grp", axis=1, tiled=True),
        lax.all_gather(w_up, "grp", axis=1, tiled=True),
        lax.all_gather(w_down, "grp", axis=2, tiled=True),
    )
    gate_full = gate_full[0]
    up_full = up_full[0]
    down_full = down_full[0]
    hidden_recv, cot_recv = (
        lax.all_to_all(hidden_send, "ep", split_axis=0, concat_axis=0, tiled=True),
        lax.all_to_all(cot_send, "ep", split_axis=0, concat_axis=0, tiled=True),
    )
    hidden_recv = hidden_recv.reshape(-1, width)
    cot_recv = cot_recv.reshape(-1, width)
    pre_gate, pre_up = forward_part(hidden_recv, gate_full, up_full)
    d_hidden, part_up, part_down = backward_part(
        hidden_recv, cot_recv, pre_gate, pre_up, gate_full, up_full, down_full
    )
    returned = lax.all_to_all(
        d_hidden.reshape(-1, capacity, width), "ep", split_axis=0, concat_axis=0, tiled=True
    )
    returned = returned.reshape(expert_count * capacity, width)
    d_normed = jnp.sum(
        returned[target].astype(jnp.float32).reshape(row_count, top_count, width), axis=1
    )
    d_scaled = d_normed * norm_gain[None, :]
    dot_mean = jnp.mean(d_scaled * normed, axis=1, keepdims=True)
    grad_tokens = (inverse * (d_scaled - normed * dot_mean)).astype(jnp.bfloat16)
    grad_up, grad_down = (
        lax.psum_scatter(
            part_up.astype(jnp.bfloat16), "grp", scatter_dimension=0, tiled=True
        ).astype(jnp.float32),
        lax.psum_scatter(
            part_down.astype(jnp.bfloat16), "grp", scatter_dimension=1, tiled=True
        ).astype(jnp.float32),
    )
    factor = 1.0 / math.sqrt(
        row_count * lax.axis_size("grp") * lax.axis_size("ep") * top_count / expert_count
    )
    return (grad_tokens, (grad_up * factor)[None], (grad_down * factor)[None])


def solution(mesh):
    in_specs = (
        P(("grp", "ep"), None),
        P(),
        P("ep", "grp", None),
        P("ep", "grp", None),
        P("ep", None, "grp"),
        P(("grp", "ep"), None),
        P(("grp", "ep"), None),
        P(("grp", "ep"), None),
    )
    out_specs = (P(("grp", "ep"), None), P("ep", "grp", None), P("ep", None, "grp"))
    return jax.shard_map(shards, mesh=mesh, in_specs=in_specs, out_specs=out_specs, check_vma=False)
```

profile of v0, /device:TPU:0, one launch (start us, length us, event | category | flops | bytes accessed | tf_op | source)
XLA Modules:
  0.0 249.7 jit_solution(9150514420220913010)
XLA Ops:
  8.0 0.7 all-gather.6.cloned.1.call-update
  9.4 0.8 copy.13
  12.4 1.4 scatter_custom_fusion
  14.3 3.1 %gather_fusion.1 = bf16[384,2048]{1,0:T(8,128)(2,1)} fusion(bf16[129,2048]{1,0:T(8,128)(2,1)S(1)} %concatenate.7, s32[1024]{0:T(1024)S(1)} %get-tuple-element.7), kind=kCustom, calls=%fused_computation.1 | custom fusion | bytes 3147264 | tf_op jit(solution)/shard_map/gather | solution.py:57
  17.4 5.3 %all-to-all-start.1 = ((bf16[8,48,2048]{2,1,0:T(8,128)(2,1)}), bf16[8,48,2048]{2,1,0:T(8,128)(2,1)}, u32[]{:S(2)}, u32[]{:S(2)}) async-start(bf16[8,48,2048]{2,1,0:T(8,128)(2,1)} %bitcast.7), calls=%async_computation.1 | async-start | bytes 3145728 | tf_op jit(solution)/shard_map/all_to_all | solution.py:68
  22.7 1.0 mul.110
  23.7 2.5 mul.111
  26.5 1.8 multiply_convert_fusion
  28.4 3.1 %gather_fusion = bf16[384,2048]{1,0:T(8,128)(2,1)} fusion(bf16[257,2048]{1,0:T(8,128)(2,1)S(1)} %concatenate.6, s32[1024]{0:T(1024)S(1)} %get-tuple-element.8), kind=kCustom, calls=%fused_computation | custom fusion | bytes 3147264 | tf_op jit(solution)/shard_map/gather | solution.py:58
  31.5 12.3 %all-to-all-done.1 = bf16[8,48,2048]{2,1,0:T(8,128)(2,1)} async-done(((bf16[8,48,2048]{2,1,0:T(8,128)(2,1)}), bf16[8,48,2048]{2,1,0:T(8,128)(2,1)}, u32[]{:S(2)}, u32[]{:S(2)}) %all-to-all-start.1) | async-done | bytes 1572896 | tf_op jit(solution)/shard_map/all_to_all | solution.py:68
  43.8 3.6 %all-to-all-start = ((bf16[8,48,2048]{2,1,0:T(8,128)(2,1)}), bf16[8,48,2048]{2,1,0:T(8,128)(2,1)S(1)}, u32[]{:S(2)}, u32[]{:S(2)}) async-start(bf16[8,48,2048]{2,1,0:T(8,128)(2,1)} %bitcast.4), calls=%async_computation | async-start | bytes 3145728 | tf_op jit(solution)/shard_map/all_to_all | solution.py:69
  47.5 10.8 %all-gather.8.cloned.1.call-done = bf16[1,2048,512]{2,1,0:T(8,128)(2,1)} async-done(((bf16[1,512,512]{2,1,0:T(8,128)(2,1)}), bf16[1,2048,512]{2,1,0:T(8,128)(2,1)}) %all-gather.8.cloned.1.call-update) | async-done | bytes 2097168 | tf_op jit(solution)/shard_map/all_gather | solution.py:60
  58.3 3.0 %fusion.2 = f32[384,512]{1,0:T(8,128)S(1)} fusion(bf16[384,2048]{1,0:T(8,128)(2,1)} %bitcast.8, bf16[1,2048,512]{2,1,0:T(8,128)(2,1)} %all-gather.8.cloned.1.call-done), kind=kOutput, calls=%fused_computation.9 | convolution fusion | flops 805306368 | bytes 4456448 | tf_op jit(solution)/shard_map/dot_general | solution.py:12
  61.3 43.2 %all-gather.6.cloned.1.call-done = bf16[1,2048,512]{2,1,0:T(8,128)(2,1)} async-done(((bf16[1,512,512]{2,1,0:T(8,128)(2,1)}), bf16[1,2048,512]{2,1,0:T(8,128)(2,1)}) %all-gather.6.cloned.1.call-update) | async-done | bytes 2097168 | tf_op jit(solution)/shard_map/all_gather | solution.py:61
  104.5 3.9 %fusion.5 = f32[384,512]{1,0:T(8,128)} fusion(bf16[384,2048]{1,0:T(8,128)(2,1)} %bitcast.8, bf16[1,2048,512]{2,1,0:T(8,128)(2,1)} %all-gather.6.cloned.1.call-done), kind=kOutput, calls=%fused_computation.12 | convolution fusion | flops 805306368 | bytes 4456448 | tf_op jit(solution)/shard_map/dot_general | solution.py:13
  108.5 3.8 %convolution_convert_fusion = bf16[512,2048]{1,0:T(8,128)(2,1)} fusion(bf16[384,2048]{1,0:T(8,128)(2,1)S(1)} %bitcast.41, f32[384,512]{1,0:T(8,128)} %fusion.5, f32[384,512]{1,0:T(8,128)S(1)} %fusion.2), kind=kOutput, calls=%fused_computation.5 | convolution fusion | flops 807534592 | bytes 5242880 | tf_op jit(solution)/shard_map/rf,rd->fd/dot_general | solution.py:31
  112.5 38.2 %all-gather.4.cloned.1.call-done = bf16[1,512,2048]{2,1,0:T(8,128)(2,1)} async-done(((bf16[1,512,512]{2,1,0:T(8,128)(2,1)}), bf16[1,512,2048]{2,1,0:T(8,128)(2,1)}) %all-gather.4.cloned.1.call-update) | async-done | bytes 2097168 | tf_op jit(solution)/shard_map/all_gather | solution.py:62
  150.8 3.7 %multiply_convert_fusion.2 = (bf16[384,512]{1,0:T(8,128)(2,1)S(1)}, f32[384,512]{1,0:T(8,128)}) fusion(f32[384,512]{1,0:T(8,128)} %copy-done.5, bf16[384,2048]{1,0:T(8,128)(2,1)S(1)} %bitcast.42, bf16[1,512,2048]{2,1,0:T(8,128)(2,1)} %all-gather.4.cloned.1.call-done), kind=kOutput, calls=%fused_computation.31 | convolution fusion | flops 806486016 | bytes 5636096 | tf_op jit(solution)/shard_map/rd,fd->rf/dot_general | solution.py:21
  154.4 4.0 %convolution_convert_fusion.1 = bf16[2048,512]{1,0:T(8,128)(2,1)} fusion(bf16[384,2048]{1,0:T(8,128)(2,1)} %bitcast.8, bf16[384,512]{1,0:T(8,128)(2,1)S(1)} %get-tuple-element.5), kind=kOutput, calls=%fused_computation.6 | convolution fusion | flops 806354944 | bytes 4063232 | tf_op jit(solution)/shard_map/rd,rf->df/dot_general | solution.py:30
  158.5 1.1 copy-done.6
  159.8 3.2 %fusion = f32[384,2048]{1,0:T(8,128)S(1)} fusion(bf16[1,2048,512]{2,1,0:T(8,128)(2,1)} %all-gather.8.cloned.1.call-done, f32[384,512]{1,0:T(8,128)S(1)} %copy-done.6, f32[384,512]{1,0:T(8,128)} %get-tuple-element.6, f32[384,512]{1,0:T(8,128)S(1)} %copy-done.7), kind=kOutput, calls=%fused_computation.7 | convolution fusion | flops 807272448 | bytes 7602176 | tf_op jit(solution)/shard_map/rf,df->rd/dot_general | solution.py:26
  163.0 2.2 add_convert_fusion
  165.2 3.7 %all-to-all-start.2 = ((bf16[8,48,2048]{2,1,0:T(8,128)(2,1)}), bf16[8,48,2048]{2,1,0:T(8,128)(2,1)S(1)}, u32[]{:S(2)}, u32[]{:S(2)}) async-start(bf16[8,48,2048]{2,1,0:T(8,128)(2,1)} %bitcast.11), calls=%async_computation.2 | async-start | bytes 3145728 | tf_op jit(solution)/shard_map/all_to_all | solution.py:77
  168.9 21.0 %all-to-all-done.2 = bf16[8,48,2048]{2,1,0:T(8,128)(2,1)S(1)} async-done(((bf16[8,48,2048]{2,1,0:T(8,128)(2,1)}), bf16[8,48,2048]{2,1,0:T(8,128)(2,1)S(1)}, u32[]{:S(2)}, u32[]{:S(2)}) %all-to-all-start.2) | async-done | bytes 1572896 | tf_op jit(solution)/shard_map/all_to_all | solution.py:77
  189.9 2.3 gather_fusion.2
  192.3 2.4 reshape.102
  194.7 2.8 %reduce_sum.41 = f32[128,2048]{1,0:T(8,128)S(1)} reduce(f32[128,2,2048]{2,1,0:T(2,128)S(1)} %reshape.102, f32[]{:T(128)} %constant.14.clone.1), dimensions={1}, to_apply=%region_5.6 | reduce | flops 262144 | bytes 3145732 | tf_op jit(solution)/shard_map/reduce_sum | solution.py:81
  197.4 1.3 fusion.13
  198.8 2.2 fusion.16
  200.9 2.2 multiply_bitcast_fusion
  203.1 37.9 %reduce-scatter.3.cloned.1.call-done = bf16[512,512]{1,0:T(8,128)(2,1)} async-done(((bf16[2048,512]{1,0:T(8,128)(2,1)}), bf16[512,512]{1,0:T(8,128)(2,1)}) %reduce-scatter.3.cloned.1.call-update) | async-done | bytes 524304 | tf_op jit(solution)/shard_map/reduce_scatter | solution.py:88
  241.0 2.2 multiply_bitcast_fusion.1
  (50 shorter events, 5.0 us)
Async XLA Ops:
  7.2 6.6 %copy-start = (bf16[128,2048]{1,0:T(8,128)(2,1)S(1)}, bf16[128,2048]{1,0:T(8,128)(2,1)}, u32[]{:S(2)}) copy-start(bf16[128,2048]{1,0:T(8,128)(2,1)} %param.8) | copy-start | bytes 1572868
  7.2 6.8 %copy-start.3 = (f32[2048]{0:T(1024)S(1)}, f32[2048]{0:T(1024)}, u32[]{:S(2)}) copy-start(f32[2048]{0:T(1024)} %param.9) | copy-start | bytes 24580
  7.2 51.1 %all-gather.8.cloned.1.call-start = ((), (), s32[]{:S(2)}) async-start(), calls=%async_computation.7 | async-start | bytes 2621440 | tf_op jit(solution)/shard_map/all_gather | solution.py:60
  7.9 96.6 %all-gather.6.cloned.1.call-start = ((), (), s32[]{:S(2)}) async-start(), calls=%async_computation.6 | async-start | bytes 2621440 | tf_op jit(solution)/shard_map/all_gather | solution.py:61
  8.7 142.1 %all-gather.4.cloned.1.call-start = ((), (), s32[]{:S(2)}) async-start(), calls=%async_computation.5 | async-start | bytes 2621440 | tf_op jit(solution)/shard_map/all_gather | solution.py:62
  17.4 5.3 %copy-start.2 = (bf16[128,2048]{1,0:T(8,128)(2,1)S(1)}, bf16[128,2048]{1,0:T(8,128)(2,1)}, u32[]{:S(2)}) copy-start(bf16[128,2048]{1,0:T(8,128)(2,1)} %param.15) | copy-start | bytes 1572868
  17.4 26.4 %all-to-all-start.1 = ((bf16[8,48,2048]{2,1,0:T(8,128)(2,1)}), bf16[8,48,2048]{2,1,0:T(8,128)(2,1)}, u32[]{:S(2)}, u32[]{:S(2)}) async-start(bf16[8,48,2048]{2,1,0:T(8,128)(2,1)} %bitcast.7), calls=%async_computation.1 | async-start | bytes 3145728 | tf_op jit(solution)/shard_map/all_to_all | solution.py:68
  23.7 2.5 copy-start.4
  43.8 64.6 %all-to-all-start = ((bf16[8,48,2048]{2,1,0:T(8,128)(2,1)}), bf16[8,48,2048]{2,1,0:T(8,128)(2,1)S(1)}, u32[]{:S(2)}, u32[]{:S(2)}) async-start(bf16[8,48,2048]{2,1,0:T(8,128)(2,1)} %bitcast.4), calls=%async_computation | async-start | bytes 3145728 | tf_op jit(solution)/shard_map/all_to_all | solution.py:69
  47.4 153.5 %reduce-scatter.5.cloned.1.call-start = ((), (), s32[]{:S(2)}) async-start(), calls=%async_computation.9 | async-start | bytes 2621440 | tf_op jit(solution)/shard_map/reduce_scatter | solution.py:91
  61.3 47.1 %copy-start.5 = (f32[384,512]{1,0:T(8,128)}, f32[384,512]{1,0:T(8,128)S(1)}, u32[]{:S(2)}) copy-start(f32[384,512]{1,0:T(8,128)S(1)} %fusion.2) | copy-start | bytes 2359300
  112.3 128.7 %reduce-scatter.3.cloned.1.call-start = ((), (), s32[]{:S(2)}) async-start(), calls=%async_computation.8 | async-start | bytes 2621440 | tf_op jit(solution)/shard_map/reduce_scatter | solution.py:88
  158.5 1.1 copy-start.6
  158.5 1.4 copy-start.7
  159.8 3.2 %copy-start.1 = (bf16[1,2048,512]{2,1,0:T(8,128)(2,1)S(1)}, bf16[1,2048,512]{2,1,0:T(8,128)(2,1)}, u32[]{:S(2)}) copy-start(bf16[1,2048,512]{2,1,0:T(8,128)(2,1)} %all-gather.6.cloned.1.call-done) | copy-start | bytes 6291460
  165.2 24.7 %all-to-all-start.2 = ((bf16[8,48,2048]{2,1,0:T(8,128)(2,1)}), bf16[8,48,2048]{2,1,0:T(8,128)(2,1)S(1)}, u32[]{:S(2)}, u32[]{:S(2)}) async-start(bf16[8,48,2048]{2,1,0:T(8,128)(2,1)} %bitcast.11), calls=%async_computation.2 | async-start | bytes 3145728 | tf_op jit(solution)/shard_map/all_to_all | solution.py:77
Sparse Core Ops, SparseCore 0:
  9.6 48.6 all-gather.7
  59.8 44.6 all-gather.5
  106.1 44.6 all-gather.3
  152.9 42.5 reduce-scatter.4
  197.8 43.1 reduce-scatter.2
where the time goes:
time: 250 us
  waiting for transfers between devices  166 us (66%)
  matrix products  23.9 us (10%)
  local copies, waits for them, and re-layouts  19.1 us (8%)
  other arithmetic  14.2 us (6%)
  between operations  14 us (6%)
  starting transfers between devices  12.9 us (5%)
    all_gather x1, waiting for transfers between devices, shards(): lax.all_gather(w_up, 'grp', axis=1, tiled=True)  43.2 us
    all_gather x1, waiting for transfers between devices, shards(): lax.all_gather(w_down, 'grp', axis=2, tiled=True)  38.2 us
    reduce_scatter x1, waiting for transfers between devices, shards(): lax.psum_scatter(part_up.astype(jnp.bfloat16), 'grp', scatter_dimension=0...  37.9 us
    all_to_all x1, waiting for transfers between devices, shards(): lax.all_to_all(d_hidden.reshape(-1, capacity, width), 'ep', split_axis=0,...  21 us
    all_to_all x1, waiting for transfers between devices, shards(): lax.all_to_all(hidden_send, 'ep', split_axis=0, concat_axis=0, tiled=True)  12.3 us
    all_gather x1, waiting for transfers between devices, shards(): lax.all_gather(w_gate, 'grp', axis=1, tiled=True)  10.8 us
    all_to_all x1, starting transfers between devices, shards(): lax.all_to_all(hidden_send, 'ep', split_axis=0, concat_axis=0, tiled=True)  5.3 us
  transfers between devices with their start and end apart: 8, of which 6 were waited for; matrix products, arithmetic and copies ran while one was open for 21% of the time, Pallas kernels for 0%

commit v1 on v0

v1 whole, which is shorter than its diff:
```python
import functools
import math

import jax
import jax.numpy as jnp
from jax import lax
from jax.experimental import pallas as pl
from jax.experimental.pallas import tpu as pltpu
from jax.sharding import PartitionSpec as P

EPS = 1e-06
F32 = jnp.float32
BF16 = jnp.bfloat16


def dot(a, b, ca, cb):
    return lax.dot_general(a, b, (((ca,), (cb,)), ((), ())), preferred_element_type=F32)


def kernel(
    grp_n, ep_n, slots_each, chunks, factor,
    tok, gain, wg, wu, wd, ids, probs, cot_in,
    gt, gu, gd,
    wgu_all, wd_all, h_send, c_send, h_recv, c_recv, d_send, d_recv,
    gates, ups, normed_s, inv_s, pick_s, own_up, own_down, left_up, left_down, right_up, right_down,
    ag_send, ag_recv, rs_send, rs_recv, h_ss, h_rs, c_ss, c_rs, d_ss, d_rs,
):
    g, me = lax.axis_index("grp"), lax.axis_index("ep")
    rows, width = tok.shape
    deep = width // grp_n
    fc = wg.shape[1] // chunks
    slots = ep_n * slots_each
    last = grp_n - 1
    right, left = lax.rem(g + 1, grp_n), lax.rem(g + grp_n - 1, grp_n)

    barrier = pltpu.get_barrier_semaphore()

    def greet(e_id, g_id):
        pl.semaphore_signal(
            barrier, inc=1, device_id=(g_id, e_id), device_id_type=pl.DeviceIdType.MESH
        )

    for d in range(1, ep_n):
        greet(lax.rem(me + d, ep_n), g)
    pl.when(g < last)(lambda: greet(me, right))
    pl.when(g > 0)(lambda: greet(me, left))
    beside = (g < last).astype(jnp.int32) + (g > 0).astype(jnp.int32)
    pl.semaphore_wait(barrier, ep_n - 1 + beside)

    def remote(src, dst, ss, rs, g_id, e_id):
        return pltpu.make_async_remote_copy(
            src_ref=src, dst_ref=dst, send_sem=ss, recv_sem=rs,
            device_id=(g_id, e_id), device_id_type=pl.DeviceIdType.MESH,
        )

    def weight_copies(c, j, way):
        to = left if way else right
        return [
            remote(buf.at[c, j], buf.at[c, j], ag_send.at[way, c, j, m], ag_recv.at[c, j, m], to, me)
            for m, buf in enumerate((wgu_all, wd_all))
        ]

    def go(copies):
        for copy in copies:
            copy.start()

    def landed(copies):
        for copy in copies:
            copy.wait_recv()

    def gone(copies):
        for copy in copies:
            copy.wait_send()

    def own_shard(c):
        pl.when(g < last)(lambda: go(weight_copies(c, g, 0)))
        pl.when(g > 0)(lambda: go(weight_copies(c, g, 1)))

    for c in range(chunks):
        cols = slice(c * fc, (c + 1) * fc)
        wgu_all[c, g, 0] = wg[:, cols]
        wgu_all[c, g, 1] = wu[:, cols]
        wd_all[c, g] = wd[cols, :]
        if c < 2:
            own_shard(c)

    id0, id1 = ids[0:1, :], ids[1:2, :]
    experts = lax.broadcasted_iota(jnp.int32, (ep_n, rows), 0)
    hit0, hit1 = (experts == id0).astype(F32), (experts == id1).astype(F32)
    before = lax.broadcasted_iota(jnp.int32, (rows, rows), 0) < lax.broadcasted_iota(
        jnp.int32, (rows, rows), 1
    )
    rank = dot((hit0 + hit1).astype(BF16), before.astype(F32).astype(BF16), 1, 0)
    at0 = id0 * slots_each + jnp.sum(hit0 * rank, axis=0, keepdims=True).astype(jnp.int32)
    at1 = id1 * slots_each + jnp.sum(hit1 * rank, axis=0, keepdims=True).astype(jnp.int32)
    slot = lax.broadcasted_iota(jnp.int32, (slots, rows), 0)
    pick0, pick1 = (slot == at0).astype(F32), (slot == at1).astype(F32)
    pick = (pick0 + pick1).astype(BF16)
    pick_s[...] = pick
    slot_prob = jnp.sum(pick0 * probs[0:1, :] + pick1 * probs[1:2, :], axis=1, keepdims=True)

    token_f = tok[...].astype(F32)
    inverse = lax.rsqrt(jnp.mean(token_f * token_f, axis=1, keepdims=True) + EPS)
    inv_s[...] = jnp.broadcast_to(inverse, inv_s.shape)
    for j in range(grp_n):
        cols = slice(j * deep, (j + 1) * deep)
        normed = tok[:, cols].astype(F32) * inverse
        normed_s[j] = normed
        hidden = (normed * gain[:, cols]).astype(BF16)
        h_send[j] = dot(pick, hidden, 1, 0).astype(BF16)
        c_send[j] = (dot(pick, cot_in[:, cols], 1, 0) * slot_prob).astype(BF16)

    def row_slots(p):
        return pl.ds(pl.multiple_of(p * slots_each, 16), slots_each)

    def exchange(src, dst, ss, rs):
        def out(d):
            p = lax.rem(me + d, ep_n)
            return remote(src.at[:, row_slots(p), :], dst.at[:, row_slots(me), :], ss.at[p], rs.at[me], g, p)

        def back(d):
            p = lax.rem(me + d, ep_n)
            return remote(src.at[:, row_slots(p), :], dst.at[:, row_slots(p), :], ss.at[p], rs.at[p], g, p)

        def start():
            lax.fori_loop(1, ep_n, lambda d, _: (out(d).start(), 0)[1], 0)
            dst[:, row_slots(me), :] = src[:, row_slots(me), :]

        def arrived():
            lax.fori_loop(1, ep_n, lambda d, _: (back(d).wait_recv(), 0)[1], 0)

        def sent():
            lax.fori_loop(1, ep_n, lambda d, _: (out(d).wait_send(), 0)[1], 0)

        return start, arrived, sent

    h_start, h_arrived, h_sent = exchange(h_send, h_recv, h_ss, h_rs)
    c_start, c_arrived, c_sent = exchange(c_send, c_recv, c_ss, c_rs)
    d_start, d_arrived, d_sent = exchange(d_send, d_recv, d_ss, d_rs)
    h_start()
    c_start()

    def gather(c):
        def step(s, _):
            from_left, from_right = g - 1 - s, g + 1 + s

            @pl.when(from_left >= 0)
            def _():
                landed(weight_copies(c, from_left, 0))
                pl.when(g < last)(lambda: go(weight_copies(c, from_left, 0)))

            @pl.when(from_right < grp_n)
            def _():
                landed(weight_copies(c, from_right, 1))
                pl.when(g > 0)(lambda: go(weight_copies(c, from_right, 1)))

            return 0

        lax.fori_loop(0, last, step, 0)

    def sum_copies(c, j, way):
        to = left if way else right
        lands = (right_up, right_down) if way else (left_up, left_down)
        return [
            remote(src.at[c, j], dst.at[c, j], rs_send.at[c, j, m], rs_recv.at[way, c, j, m], to, me)
            for m, (src, dst) in enumerate(zip((own_up, own_down), lands))
        ]

    def compute(c):
        pre_gate = jnp.zeros((slots, fc), F32)
        pre_up = jnp.zeros((slots, fc), F32)
        d_swiglu = jnp.zeros((slots, fc), F32)
        for j in range(grp_n):
            pre_gate += dot(h_recv[j], wgu_all[c, j, 0], 1, 0)
            pre_up += dot(h_recv[j], wgu_all[c, j, 1], 1, 0)
            d_swiglu += dot(c_recv[j], wd_all[c, j], 1, 1)
        sig = jax.nn.sigmoid(pre_gate)
        act = pre_gate * sig
        swiglu = (act * pre_up).astype(BF16)
        d_up = (d_swiglu * act).astype(BF16)
        gates[c] = (d_swiglu * pre_up * sig * (1.0 + pre_gate * (1.0 - sig))).astype(BF16)
        ups[c] = d_up

        def part(j):
            own_up[c, j] = dot(h_recv[j], d_up, 0, 0).astype(BF16)
            own_down[c, j] = dot(swiglu, c_recv[j], 0, 0).astype(BF16)

        def step(i, _):
            far = last - i

            @pl.when(g + far < grp_n)
            def _():
                part(g + far)
                pl.when(jnp.logical_and(g == 0, far > 0))(lambda: go(sum_copies(c, g + far, 0)))

            @pl.when(jnp.logical_and(g - far >= 0, far > 0))
            def _():
                part(g - far)
                pl.when(g == last)(lambda: go(sum_copies(c, g - far, 1)))

            return 0

        lax.fori_loop(0, grp_n, step, 0)

    def reduce(c):
        def add(j, lands):
            own_up[c, j] = (own_up[c, j].astype(F32) + lands[0][c, j].astype(F32)).astype(BF16)
            own_down[c, j] = (own_down[c, j].astype(F32) + lands[1][c, j].astype(F32)).astype(BF16)

        def step(i, _):
            far = last - i

            @pl.when(jnp.logical_and(g + far < grp_n, g > 0))
            def _():
                landed(sum_copies(c, g + far, 0))
                add(g + far, (left_up, left_down))
                go(sum_copies(c, g + far, 0))

            @pl.when(jnp.logical_and(g - far >= 0, g < last))
            def _():
                landed(sum_copies(c, g - far, 1))
                add(g - far, (right_up, right_down))
                go(sum_copies(c, g - far, 1))

            return 0

        lax.fori_loop(0, last, step, 0)
        cols = pl.ds(pl.multiple_of(c * fc, fc), fc)
        gu[:, cols] = own_up[c, g].astype(F32)
        gd[cols, :] = own_down[c, g].astype(F32)

        @pl.when(g > 0)
        def _():
            landed(sum_copies(c, g, 0))
            gu[:, cols] += left_up[c, g].astype(F32)
            gd[cols, :] += left_down[c, g].astype(F32)

        @pl.when(g < last)
        def _():
            landed(sum_copies(c, g, 1))
            gu[:, cols] += right_up[c, g].astype(F32)
            gd[cols, :] += right_down[c, g].astype(F32)

        gu[:, cols] *= factor
        gd[cols, :] *= factor

    def chunk(c, _):
        gather(c)
        pl.when(c + 2 < chunks)(lambda: own_shard(c + 2))

        @pl.when(c == 0)
        def _():
            h_arrived()
            c_arrived()

        compute(c)
        pl.when(c > 0)(lambda: reduce(c - 1))
        return 0

    lax.fori_loop(0, chunks, chunk, 0)

    def back_rows(j, _):
        total = jnp.zeros((slots, deep), F32)
        for c in range(chunks):
            total += dot(gates[c], wgu_all[c, j, 0], 1, 1)
            total += dot(ups[c], wgu_all[c, j, 1], 1, 1)
        d_send[j] = total.astype(BF16)
        return 0

    lax.fori_loop(0, grp_n, back_rows, 0)
    d_start()
    reduce(chunks - 1)
    d_arrived()

    pick = pick_s[...]
    inverse = inv_s[:, 0:1]
    mean = jnp.zeros((rows, 1), F32)
    scaled = []
    for j in range(grp_n):
        cols = slice(j * deep, (j + 1) * deep)
        s = dot(pick, d_recv[j], 0, 0) * gain[:, cols]
        mean += jnp.sum(s * normed_s[j], axis=1, keepdims=True)
        scaled.append(s)
    mean = mean * (1.0 / width)
    for j in range(grp_n):
        cols = slice(j * deep, (j + 1) * deep)
        gt[:, cols] = (inverse * (scaled[j] - normed_s[j] * mean)).astype(BF16)

    h_sent()
    c_sent()
    d_sent()

    def drain(i, _):
        c, j = i // grp_n, lax.rem(i, grp_n)
        pl.when(jnp.logical_and(j <= g, g < last))(lambda: gone(weight_copies(c, j, 0)))
        pl.when(jnp.logical_and(j >= g, g > 0))(lambda: gone(weight_copies(c, j, 1)))
        pl.when(j > g)(lambda: gone(sum_copies(c, j, 0)))
        pl.when(j < g)(lambda: gone(sum_copies(c, j, 1)))
        return 0

    lax.fori_loop(0, chunks * grp_n, drain, 0)


def shards(grp_n, ep_n, tokens, norm_gain, w_gate, w_up, w_down, expert_ids, probs, out_grad):
    rows, width = tokens.shape
    top = expert_ids.shape[1]
    inner = w_gate.shape[2]
    capacity = max(2, 3 * rows * top // (2 * ep_n))
    slots_each = -(-capacity // 16) * 16
    slots = ep_n * slots_each
    deep = width // grp_n
    chunks = inner // 128
    fc = inner // chunks
    factor = 1.0 / math.sqrt(rows * grp_n * ep_n * top / ep_n)
    dma = pltpu.SemaphoreType.DMA
    wide = [pltpu.VMEM((grp_n, slots, deep), BF16)] * 6
    ups, downs = pltpu.VMEM((chunks, grp_n, deep, fc), BF16), pltpu.VMEM((chunks, grp_n, fc, deep), BF16)
    vmem = pl.BlockSpec(memory_space=pltpu.VMEM)
    grad_tokens, grad_up, grad_down = pl.pallas_call(
        functools.partial(kernel, grp_n, ep_n, slots_each, chunks, factor),
        out_shape=(
            jax.ShapeDtypeStruct((rows, width), BF16),
            jax.ShapeDtypeStruct((deep, inner), F32),
            jax.ShapeDtypeStruct((inner, deep), F32),
        ),
        in_specs=[vmem] * 8,
        out_specs=(vmem, vmem, vmem),
        scratch_shapes=[
            pltpu.VMEM((chunks, grp_n, 2, deep, fc), BF16),
            downs,
            *wide,
            pltpu.VMEM((chunks, slots, fc), BF16),
            pltpu.VMEM((chunks, slots, fc), BF16),
            pltpu.VMEM((grp_n, rows, deep), F32),
            pltpu.VMEM((rows, 128), F32),
            pltpu.VMEM((slots, rows), BF16),
            ups, downs, ups, downs, ups, downs,
            dma((2, chunks, grp_n, 2)), dma((chunks, grp_n, 2)),
            dma((chunks, grp_n, 2)), dma((2, chunks, grp_n, 2)),
            dma((ep_n,)), dma((ep_n,)), dma((ep_n,)), dma((ep_n,)), dma((ep_n,)), dma((ep_n,)),
        ],
        compiler_params=pltpu.CompilerParams(
            collective_id=0, has_side_effects=True, vmem_limit_bytes=56 * 2**20
        ),
    )(
        tokens, norm_gain[None, :], w_gate[0], w_up[0], w_down[0], expert_ids.T, probs.T, out_grad,
    )
    return grad_tokens, grad_up[None], grad_down[None]


def solution(mesh):
    in_specs = (
        P(("grp", "ep"), None),
        P(),
        P("ep", "grp", None),
        P("ep", "grp", None),
        P("ep", None, "grp"),
        P(("grp", "ep"), None),
        P(("grp", "ep"), None),
        P(("grp", "ep"), None),
    )
    out_specs = (P(("grp", "ep"), None), P("ep", "grp", None), P("ep", None, "grp"))
    return jax.shard_map(
        functools.partial(shards, mesh.shape["grp"], mesh.shape["ep"]),
        mesh=mesh, in_specs=in_specs, out_specs=out_specs, check_vma=False,
    )
```

time: 250 us -> 159 us (0.64)
  waiting for transfers between devices: 166 us -> 0 us
  Pallas kernels: 0 us -> 153 us
  matrix products: 23.9 us -> 0 us
  local copies, waits for them, and re-layouts: 19.1 us -> 4.55 us
  other arithmetic: 14.2 us -> 0 us
  between operations: 14 us -> 0.65 us
  starting transfers between devices: 12.9 us -> 0 us
    pallas_call x0 -> x1, Pallas kernels: none -> 153 us  [shards(): pl.pallas_call(functools.partial(kernel, grp_n, ep_n, slots_each, chunks,...]
    all_gather x3 -> x0, waiting for transfers between devices: 92.3 us -> none  [the longest x1 43.2 us: shards(): lax.all_gather(w_up, 'grp', axis=1, tiled=True)]
    reduce_scatter x2 -> x0, waiting for transfers between devices: 37.9 us -> none  [the longest x1 37.9 us: shards(): lax.psum_scatter(part_up.astype(jnp.bfloat16), 'grp', scatter_dimension=0...]
    all_to_all x3 -> x0, waiting for transfers between devices: 33.4 us -> none  [the longest x1 21 us: shards(): lax.all_to_all(d_hidden.reshape(-1, capacity, width), 'ep', split_axis=0,...]
    dot_general x7 -> x0, matrix products: 23.9 us -> none  [the longest x1 4.01 us: backward_part(): jnp.einsum('rd,rf->df', hidden_rows, d_up_pre, preferred_element_type=jnp...]
    all_to_all x3 -> x0, starting transfers between devices: 12.5 us -> none  [the longest x1 5.3 us: shards(): lax.all_to_all(hidden_send, 'ep', split_axis=0, concat_axis=0, tiled=True)]
    gather x3 -> x0, local copies, waits for them, and re-layouts: 8.54 us -> none  [the longest x1 3.12 us: shards(): hidden_pad[source // top_count].reshape(expert_count, capacity, width)]
    reduce_sum x4 -> x0, other arithmetic: 4.38 us -> none  [the longest x1 2.76 us: shards(): jnp.sum(returned[target].astype(jnp.float32).reshape(row_count, top_count...]
  transfers between devices with their start and end apart: 8 -> 0, of which waited for: 6 -> 0; matrix products, arithmetic and copies ran while one was open for 21% -> 0% of each run, Pallas kernels for 0% -> 0%
where the time goes in v1:
time: 159 us; the launch traced here: 158 us
  Pallas kernels  153 us (96%)
  local copies, waits for them, and re-layouts  4.55 us (3%)
    pallas_call x1, Pallas kernels, shards(): pl.pallas_call(functools.partial(kernel, grp_n, ep_n, slots_each, chunks,...  153 us
    unnamed x7, local copies, waits for them, and re-layouts  4.55 us

profile of v1, /device:TPU:0, one launch (start us, length us, event | category | flops | bytes accessed | tf_op | source)
XLA Modules:
  0.0 157.7 jit_solution(5830397697921220551)
XLA Ops:
  0.6 152.5 %shard_map.103 = (bf16[128,2048]{1,0:T(8,128)(2,1)}, f32[512,512]{1,0:T(8,128)}, f32[512,512]{1,0:T(8,128)}) custom-call(bf16[128,2048]{1,0:T(8,128)(2,1)} %tok.1, f32[1,2048]{1,0:T(1,128)} %bitcast.13, bf16[512,512]{1,0:T(8,128)(2,1)} %bitcast.10, bf16[512,512]{1,0:T(8,128)(2,1)} %bitcast.11, bf16[512,512]{1,0:T(8,128)(2,1)} %bitcast.12, ...), custom_call_target="tpu_custom_call" | custom-call | tf_op jit(solution)/shard_map/pallas_call | solution.py:319
  153.2 0.0 copy-start.1
  153.2 2.0 %copy.14 = bf16[128,2048]{1,0:T(8,128)(2,1)} copy(bf16[128,2048]{1,0:T(8,128)(2,1)} %get-tuple-element.12) | data formatting | bytes 1048576
  155.2 0.0 copy-done.1
  155.2 0.0 copy-start
  155.2 1.0 copy.15
  156.1 0.6 copy-done
  156.8 1.0 copy.16
Async XLA Ops:
  153.2 2.0 %copy-start.1 = (f32[512,512]{1,0:T(8,128)S(1)}, f32[512,512]{1,0:T(8,128)}, u32[]{:S(2)}) copy-start(f32[512,512]{1,0:T(8,128)} %get-tuple-element.7) | copy-start | bytes 3145732
  155.2 1.6 %copy-start = (f32[512,512]{1,0:T(8,128)S(1)}, f32[512,512]{1,0:T(8,128)}, u32[]{:S(2)}) copy-start(f32[512,512]{1,0:T(8,128)} %get-tuple-element.8) | copy-start | bytes 3145732

commit v2 on v1

--- a/solution.py
+++ b/solution.py
@@ -22,7 +22,7 @@
     tok, gain, wg, wu, wd, ids, probs, cot_in,
     gt, gu, gd,
     wgu_all, wd_all, h_send, c_send, h_recv, c_recv, d_send, d_recv,
-    gates, ups, normed_s, inv_s, pick_s, own_up, own_down, left_up, left_down, right_up, right_down,
+    back_s, normed_s, inv_s, pick_s, own_up, own_down, left_up, left_down, right_up, right_down,
     ag_send, ag_recv, rs_send, rs_recv, h_ss, h_rs, c_ss, c_rs, d_ss, d_rs,
 ):
     g, me = lax.axis_index("grp"), lax.axis_index("ep")
@@ -178,8 +178,7 @@
         act = pre_gate * sig
         swiglu = (act * pre_up).astype(BF16)
         d_up = (d_swiglu * act).astype(BF16)
-        gates[c] = (d_swiglu * pre_up * sig * (1.0 + pre_gate * (1.0 - sig))).astype(BF16)
-        ups[c] = d_up
+        d_gate = (d_swiglu * pre_up * sig * (1.0 + pre_gate * (1.0 - sig))).astype(BF16)
 
         def part(j):
             own_up[c, j] = dot(h_recv[j], d_up, 0, 0).astype(BF16)
@@ -202,7 +201,26 @@
 
         lax.fori_loop(0, grp_n, step, 0)
 
-    def reduce(c):
+        def back_rows(first, final):
+            for j in range(grp_n):
+                total = dot(d_gate, wgu_all[c, j, 0], 1, 1) + dot(d_up, wgu_all[c, j, 1], 1, 1)
+                if not first:
+                    total += back_s[j]
+                if final:
+                    d_send[j] = total.astype(BF16)
+                else:
+                    back_s[j] = total
+
+        if chunks == 1:
+            back_rows(True, True)
+        else:
+            pl.when(c == 0)(lambda: back_rows(True, False))
+            pl.when(jnp.logical_and(c > 0, c < chunks - 1))(lambda: back_rows(False, False))
+            pl.when(c == chunks - 1)(lambda: back_rows(False, True))
+
+    early = g >= (grp_n + 1) // 2
+
+    def pass_on(c, way_is_left):
         def add(j, lands):
             own_up[c, j] = (own_up[c, j].astype(F32) + lands[0][c, j].astype(F32)).astype(BF16)
             own_down[c, j] = (own_down[c, j].astype(F32) + lands[1][c, j].astype(F32)).astype(BF16)
@@ -210,13 +228,16 @@
         def step(i, _):
             far = last - i
 
-            @pl.when(jnp.logical_and(g + far < grp_n, g > 0))
+            go_right = jnp.logical_and(g + far < grp_n, g > 0)
+            go_left = jnp.logical_and(g - far >= 0, g < last)
+
+            @pl.when(jnp.logical_and(go_right, jnp.logical_not(way_is_left)))
             def _():
                 landed(sum_copies(c, g + far, 0))
                 add(g + far, (left_up, left_down))
                 go(sum_copies(c, g + far, 0))
 
-            @pl.when(jnp.logical_and(g - far >= 0, g < last))
+            @pl.when(jnp.logical_and(go_left, way_is_left))
             def _():
                 landed(sum_copies(c, g - far, 1))
                 add(g - far, (right_up, right_down))
@@ -225,24 +246,33 @@
             return 0
 
         lax.fori_loop(0, last, step, 0)
+
+    def finish(c, _):
         cols = pl.ds(pl.multiple_of(c * fc, fc), fc)
-        gu[:, cols] = own_up[c, g].astype(F32)
-        gd[cols, :] = own_down[c, g].astype(F32)
-
-        @pl.when(g > 0)
+        up, down = own_up[c, g].astype(F32), own_down[c, g].astype(F32)
+
+        @pl.when(g == 0)
+        def _():
+            landed(sum_copies(c, g, 1))
+            gu[:, cols] = (up + right_up[c, g].astype(F32)) * factor
+            gd[cols, :] = (down + right_down[c, g].astype(F32)) * factor
+
+        @pl.when(g == last)
         def _():
             landed(sum_copies(c, g, 0))
-            gu[:, cols] += left_up[c, g].astype(F32)
-            gd[cols, :] += left_down[c, g].astype(F32)
-
-        @pl.when(g < last)
+            gu[:, cols] = (up + left_up[c, g].astype(F32)) * factor
+            gd[cols, :] = (down + left_down[c, g].astype(F32)) * factor
+
+        @pl.when(jnp.logical_and(g > 0, g < last))
         def _():
+            landed(sum_copies(c, g, 0))
             landed(sum_copies(c, g, 1))
-            gu[:, cols] += right_up[c, g].astype(F32)
-            gd[cols, :] += right_down[c, g].astype(F32)
-
-        gu[:, cols] *= factor
-        gd[cols, :] *= factor
+            sides = left_up[c, g].astype(F32) + right_up[c, g].astype(F32)
+            gu[:, cols] = (up + sides) * factor
+            sides = left_down[c, g].astype(F32) + right_down[c, g].astype(F32)
+            gd[cols, :] = (down + sides) * factor
+
+        return 0
 
     def chunk(c, _):
         gather(c)
@@ -254,22 +284,26 @@
             c_arrived()
 
         compute(c)
-        pl.when(c > 0)(lambda: reduce(c - 1))
+        pl.when(c > 0)(lambda: pass_on(c - 1, early))
         return 0
 
     lax.fori_loop(0, chunks, chunk, 0)
 
-    def back_rows(j, _):
-        total = jnp.zeros((slots, deep), F32)
-        for c in range(chunks):
-            total += dot(gates[c], wgu_all[c, j, 0], 1, 1)
-            total += dot(ups[c], wgu_all[c, j, 1], 1, 1)
-        d_send[j] = total.astype(BF16)
+    d_start()
+
+    def weights_left(i, _):
+        c, j = i // grp_n, lax.rem(i, grp_n)
+        right_near, left_near = jnp.logical_and(early, g < last), jnp.logical_and(jnp.logical_not(early), g > 0)
+        pl.when(jnp.logical_and(j <= g, right_near))(lambda: gone(weight_copies(c, j, 0)))
+        pl.when(jnp.logical_and(j >= g, left_near))(lambda: gone(weight_copies(c, j, 1)))
         return 0
 
-    lax.fori_loop(0, grp_n, back_rows, 0)
-    d_start()
-    reduce(chunks - 1)
+    lax.fori_loop(0, chunks * grp_n, weights_left, 0)
+    late = jnp.logical_not(early)
+    lax.fori_loop(0, chunks - 1, lambda c, _: (pass_on(c, late), 0)[1], 0)
+    pass_on(chunks - 1, early)
+    pass_on(chunks - 1, late)
+    lax.fori_loop(0, chunks - 1, finish, 0)
     d_arrived()
 
     pick = pick_s[...]
@@ -286,14 +320,17 @@
         cols = slice(j * deep, (j + 1) * deep)
         gt[:, cols] = (inverse * (scaled[j] - normed_s[j] * mean)).astype(BF16)
 
+    finish(chunks - 1, 0)
+
     h_sent()
     c_sent()
     d_sent()
 
     def drain(i, _):
         c, j = i // grp_n, lax.rem(i, grp_n)
-        pl.when(jnp.logical_and(j <= g, g < last))(lambda: gone(weight_copies(c, j, 0)))
-        pl.when(jnp.logical_and(j >= g, g > 0))(lambda: gone(weight_copies(c, j, 1)))
+        right_far, left_far = jnp.logical_and(late, g < last), jnp.logical_and(early, g > 0)
+        pl.when(jnp.logical_and(j <= g, right_far))(lambda: gone(weight_copies(c, j, 0)))
+        pl.when(jnp.logical_and(j >= g, left_far))(lambda: gone(weight_copies(c, j, 1)))
         pl.when(j > g)(lambda: gone(sum_copies(c, j, 0)))
         pl.when(j < g)(lambda: gone(sum_copies(c, j, 1)))
         return 0
@@ -329,8 +366,7 @@
             pltpu.VMEM((chunks, grp_n, 2, deep, fc), BF16),
             downs,
             *wide,
-            pltpu.VMEM((chunks, slots, fc), BF16),
-            pltpu.VMEM((chunks, slots, fc), BF16),
+            pltpu.VMEM((grp_n, slots, deep), F32),
             pltpu.VMEM((grp_n, rows, deep), F32),
             pltpu.VMEM((rows, 128), F32),
             pltpu.VMEM((slots, rows), BF16),

time: 159 us -> 149 us (0.937)
  Pallas kernels: 153 us -> 144 us
    pallas_call x1, Pallas kernels: 153 us -> 144 us  [shards(): pl.pallas_call(functools.partial(kernel, grp_n, ep_n, slots_each, chunks,...]
where the time goes in v2:
time: 149 us
  Pallas kernels  144 us (97%)
  local copies, waits for them, and re-layouts  4.55 us (3%)
    pallas_call x1, Pallas kernels, shards(): pl.pallas_call(functools.partial(kernel, grp_n, ep_n, slots_each, chunks,...  144 us
    unnamed x7, local copies, waits for them, and re-layouts  4.55 us

profile of v2, /device:TPU:0, one launch (start us, length us, event | category | flops | bytes accessed | tf_op | source)
XLA Modules:
  0.0 148.8 jit_solution(6019399797726112798)
XLA Ops:
  0.6 143.7 %shard_map.103 = (bf16[128,2048]{1,0:T(8,128)(2,1)}, f32[512,512]{1,0:T(8,128)}, f32[512,512]{1,0:T(8,128)}) custom-call(bf16[128,2048]{1,0:T(8,128)(2,1)} %tok.1, f32[1,2048]{1,0:T(1,128)} %bitcast.13, bf16[512,512]{1,0:T(8,128)(2,1)} %bitcast.10, bf16[512,512]{1,0:T(8,128)(2,1)} %bitcast.11, bf16[512,512]{1,0:T(8,128)(2,1)} %bitcast.12, ...), custom_call_target="tpu_custom_call" | custom-call | tf_op jit(solution)/shard_map/pallas_call | solution.py:356
  144.3 0.0 copy-start.1
  144.3 2.0 %copy.14 = bf16[128,2048]{1,0:T(8,128)(2,1)} copy(bf16[128,2048]{1,0:T(8,128)(2,1)} %get-tuple-element.12) | data formatting | bytes 1048576
  146.3 0.0 copy-done.1
  146.3 0.0 copy-start
  146.3 1.0 copy.15
  147.2 0.6 copy-done
  147.9 1.0 copy.16
Async XLA Ops:
  144.3 2.0 %copy-start.1 = (f32[512,512]{1,0:T(8,128)S(1)}, f32[512,512]{1,0:T(8,128)}, u32[]{:S(2)}) copy-start(f32[512,512]{1,0:T(8,128)} %get-tuple-element.7) | copy-start | bytes 3145732
  146.3 1.6 %copy-start = (f32[512,512]{1,0:T(8,128)S(1)}, f32[512,512]{1,0:T(8,128)}, u32[]{:S(2)}) copy-start(f32[512,512]{1,0:T(8,128)} %get-tuple-element.8) | copy-start | bytes 3145732

commit v3 on v2

--- a/solution.py
+++ b/solution.py
@@ -81,7 +81,7 @@
         wgu_all[c, g, 0] = wg[:, cols]
         wgu_all[c, g, 1] = wu[:, cols]
         wd_all[c, g] = wd[cols, :]
-        if c < 2:
+        if c < 3:
             own_shard(c)
 
     id0, id1 = ids[0:1, :], ids[1:2, :]
@@ -274,9 +274,12 @@
 
         return 0
 
+    inside = jnp.logical_and(g > 0, g < last)
+
     def chunk(c, _):
-        gather(c)
-        pl.when(c + 2 < chunks)(lambda: own_shard(c + 2))
+        pl.when(jnp.logical_or(c == 0, jnp.logical_not(inside)))(lambda: gather(c))
+        pl.when(jnp.logical_and(c + 1 < chunks, inside))(lambda: gather(c + 1))
+        pl.when(c + 3 < chunks)(lambda: own_shard(c + 3))
 
         @pl.when(c == 0)
         def _():

time: 149 us -> 144 us (0.966)
  Pallas kernels: 144 us -> 138 us
    pallas_call x1, Pallas kernels: 144 us -> 138 us  [shards(): pl.pallas_call(functools.partial(kernel, grp_n, ep_n, slots_each, chunks,...]
where the time goes in v3:
time: 144 us
  Pallas kernels  138 us (96%)
  local copies, waits for them, and re-layouts  4.55 us (3%)
    pallas_call x1, Pallas kernels, shards(): pl.pallas_call(functools.partial(kernel, grp_n, ep_n, slots_each, chunks,...  138 us
    unnamed x7, local copies, waits for them, and re-layouts  4.55 us

profile of v3, /device:TPU:0, one launch (start us, length us, event | category | flops | bytes accessed | tf_op | source)
XLA Modules:
  0.0 143.7 jit_solution(16807205196494143608)
XLA Ops:
  0.6 138.5 %shard_map.103 = (bf16[128,2048]{1,0:T(8,128)(2,1)}, f32[512,512]{1,0:T(8,128)}, f32[512,512]{1,0:T(8,128)}) custom-call(bf16[128,2048]{1,0:T(8,128)(2,1)} %tok.1, f32[1,2048]{1,0:T(1,128)} %bitcast.13, bf16[512,512]{1,0:T(8,128)(2,1)} %bitcast.10, bf16[512,512]{1,0:T(8,128)(2,1)} %bitcast.11, bf16[512,512]{1,0:T(8,128)(2,1)} %bitcast.12, ...), custom_call_target="tpu_custom_call" | custom-call | tf_op jit(solution)/shard_map/pallas_call | solution.py:359
  139.1 0.0 copy-start.1
  139.1 2.0 %copy.14 = bf16[128,2048]{1,0:T(8,128)(2,1)} copy(bf16[128,2048]{1,0:T(8,128)(2,1)} %get-tuple-element.12) | data formatting | bytes 1048576
  141.1 0.0 copy-done.1
  141.1 0.0 copy-start
  141.1 1.0 copy.15
  142.0 0.6 copy-done
  142.7 1.0 copy.16
Async XLA Ops:
  139.1 2.0 %copy-start.1 = (f32[512,512]{1,0:T(8,128)S(1)}, f32[512,512]{1,0:T(8,128)}, u32[]{:S(2)}) copy-start(f32[512,512]{1,0:T(8,128)} %get-tuple-element.7) | copy-start | bytes 3145732
  141.1 1.6 %copy-start = (f32[512,512]{1,0:T(8,128)S(1)}, f32[512,512]{1,0:T(8,128)}, u32[]{:S(2)}) copy-start(f32[512,512]{1,0:T(8,128)} %get-tuple-element.8) | copy-start | bytes 3145732
